TPU v7x, 32 devices: a whole 2x2x4 slice. The times are simulated.
32 devices in a mesh: groups: 2 (over x), col: 16 (over z, y, core).
Axes of the slice: x: 2, y: 2, z: 4, core: 2. Of those that a mesh axis runs over, the one named last changes fastest.
Arguments:
- features: bfloat16 [8192, 256], P(('groups', 'col')), parts along dimension 0, may hold values from -6 to 6
- block_values: bfloat16 [4096, 128, 128], P(('groups', 'col')), parts along dimension 0, may hold values from -0.09375 to 0.09375
- block_owner: int32 [4096, 1], P(('groups', 'col')), parts along dimension 0, may hold values from 0 to 15; in each aligned block of 128 rows (0 to 127, 128 to 255, ...) at most 16 rows name the same one
- block_sub: int32 [4096], P(('groups', 'col')), parts along dimension 0, may hold values from 0 to 1
- block_col: int32 [4096], P(('groups', 'col')), parts along dimension 0, may hold values from 0 to 1
- block_valid: int32 [4096], P(('groups', 'col')), parts along dimension 0, may hold values from 0 to 1, as said below
- norm_gain: float32 [256], replicated, may hold values from 0.1 to 1.9
- weight: bfloat16 [256, 256], replicated, may hold values from -0.375 to 0.375
Outputs:
- propagated: float32 [8192, 256], P(('groups', 'col')), parts along dimension 0
There are 2 independent parts, one for each index of `groups`. A program takes and returns all parts, laid end to end along the dimension named above; an argument that names none is the same for every part. Nothing has to cross between parts.
Inputs may be any that keep to these rules, and one draw needn't show every extreme that they name: `block_owner`: in the 128 slots of one tile no owner is named more than 16 times; in every draw some owner is named exactly 16 times in some tile. `block_valid`: each tile has at least 16 live slots, and in every draw some tile has all 128 slots live.
All inputs are finite; a program needn't handle non-finite values.
Results may differ from a plain program's by a relative error of at most 0.0032.
Values may be sent and summed in bfloat16 or wider, within the bound.
A program may use at most 128 MiB of HBM per device.

v0:
```python
import jax
import jax.numpy as jnp
from jax import lax
from jax.sharding import PartitionSpec as P


def body(features, block_values, block_owner, block_sub, block_col, block_valid, norm_gain, weight):
    block_size = block_values.shape[1]
    node_rows = features.shape[0]
    feature_width = features.shape[1]
    per_dev = node_rows // block_size
    devices = lax.axis_size("col")
    slot_owner = block_owner[:, 0]
    row_block = slot_owner * per_dev + block_sub
    live_mask = block_valid.astype(jnp.float32)
    source_rows = features.reshape(per_dev, block_size, feature_width)[block_col]
    products = jnp.einsum(
        "sab,sbf->saf", block_values, source_rows, preferred_element_type=jnp.float32
    )
    products = products * live_mask[:, None, None]
    partial_sums = jax.ops.segment_sum(products, row_block, num_segments=devices * per_dev)
    partial_sums = partial_sums.reshape(devices * node_rows, feature_width)
    aggregate = lax.psum_scatter(partial_sums, "col", scatter_dimension=0, tiled=True)
    row_scale = lax.rsqrt(jnp.mean(aggregate * aggregate, axis=1) + 1e-06)
    normed = (aggregate * row_scale[:, None] * norm_gain[None, :]).astype(jnp.bfloat16)
    hidden = jax.nn.relu(jnp.dot(normed, weight, preferred_element_type=jnp.float32)).astype(
        jnp.bfloat16
    )
    all_hidden = lax.all_gather(hidden, "col", axis=0, tiled=True)
    picked_hidden = all_hidden.reshape(-1, block_size, feature_width)[row_block]
    returned = jnp.einsum(
        "sab,saf->sbf", block_values, picked_hidden, preferred_element_type=jnp.float32
    )
    returned = returned * live_mask[:, None, None]
    result_rows = jax.ops.segment_sum(returned, block_col, num_segments=per_dev)
    return result_rows.reshape(node_rows, feature_width)


def solution(mesh):
    placed = (
        P(("groups", "col"), None),
        P(("groups", "col"), None, None),
        P(("groups", "col"), None),
        P(("groups", "col")),
        P(("groups", "col")),
        P(("groups", "col")),
        P(),
        P(),
    )
    return jax.shard_map(
        body, mesh=mesh, in_specs=placed, out_specs=P(("groups", "col"), None), check_vma=False
    )
```

profile of v0, /device:TPU:0, one launch (start us, length us, event | category | flops | bytes accessed | tf_op | source)
XLA Modules:
  0.0 275.1 jit_solution(13188056985551898893)
XLA Ops:
  6.5 0.0 copy-start
  6.5 0.0 reduce-scatter.2.cloned.1.call-start
  6.5 0.7 convert_element_type.9
  7.2 0.7 compare_select_fusion.1
  7.9 0.0 copy-done
  7.9 6.4 %gather_fusion = bf16[128,128,256]{2,1,0:T(8,128)(2,1)} fusion(bf16[2,128,256]{2,1,0:T(8,128)(2,1)S(1)} %bitcast.16, s32[1024]{0:T(1024)S(1)} %pad_clamp_fusion.1), kind=kCustom, calls=%fused_computation | custom fusion | bytes 16777728 | tf_op jit(solution)/shard_map/gather | solution.py:16
  14.3 12.9 %multiply_bitcast_fusion.1 = f32[128,128,256]{1,2,0:T(8,128)} fusion(bf16[128,128,256]{2,1,0:T(8,128)(2,1)} %gather_fusion, bf16[128,128,128]{2,1,0:T(8,128)(2,1)} %param.9, f32[128]{0:T(128)S(1)} %convert_element_type.9), kind=kOutput, calls=%fused_computation.5 | convolution fusion | flops 1077936128 | bytes 29360640 | tf_op jit(solution)/shard_map/sab,sbf->saf/dot_general | solution.py:17
  27.2 0.0 copy-start.6
  27.2 0.0 copy-start.7
  27.2 17.5 %copy.12 = f32[128,128,256]{2,1,0:T(8,128)} copy(f32[128,128,256]{1,2,0:T(8,128)} %multiply_bitcast_fusion.1) | data formatting | bytes 33554432 | tf_op jit(solution)/shard_map/mul | solution.py:20
  44.7 0.0 copy-done.6
  44.7 0.0 copy-done.7
  44.7 2.4 broadcast_in_dim.24
  47.1 0.0 copy-start.3
  47.1 0.0 copy-start.4
  47.1 37.8 %scatter_fusion = f32[32,128,256]{2,1,0:T(8,128)} fusion(f32[32,128,256]{2,1,0:T(8,128)} %broadcast_in_dim.24, s32[128]{0:T(128)S(1)} %get-tuple-element.6, f32[128,128,256]{2,1,0:T(8,128)} %copy.12), kind=kCustom, calls=%fused_computation.2 | custom fusion | flops 4194304 | bytes 50332160 | tf_op jit(solution)/shard_map/scatter-add | solution.py:21
  84.9 0.0 reduce-scatter.2.cloned.1.call-update
  85.0 0.2 all-gather.2.cloned.1.call-start
  85.2 75.3 %reduce-scatter.2.cloned.1.call-done = f32[256,256]{1,0:T(8,128)} async-done(((f32[4096,256]{1,0:T(8,128)}), f32[256,256]{1,0:T(8,128)}) %reduce-scatter.2.cloned.1.call-update) | async-done | bytes 262160 | tf_op jit(solution)/shard_map/reduce_scatter | solution.py:23
  160.5 1.1 multiply_reduce_fusion
  161.6 0.0 copy-done.3
  161.6 0.0 copy-done.4
  161.6 1.8 fusion
  163.4 0.0 all-gather.2.cloned.1.call-update
  163.5 40.7 %all-gather.2.cloned.1.call-done = bf16[4096,256]{1,0:T(8,128)(2,1)} async-done(((bf16[256,256]{1,0:T(8,128)(2,1)}), bf16[4096,256]{1,0:T(8,128)(2,1)}) %all-gather.2.cloned.1.call-update) | async-done | bytes 2097168 | tf_op jit(solution)/shard_map/all_gather | solution.py:29
  204.1 8.2 %gather_fusion.1 = bf16[128,128,256]{2,1,0:T(8,128)(2,1)} fusion(bf16[32,128,256]{2,1,0:T(8,128)(2,1)} %bitcast.18, s32[1024]{0:T(1024)S(1)} %pad_clamp_fusion), kind=kCustom, calls=%fused_computation.1 | custom fusion | bytes 16777728 | tf_op jit(solution)/shard_map/gather | solution.py:30
  212.3 13.7 %multiply_bitcast_fusion = f32[128,128,256]{1,2,0:T(8,128)} fusion(bf16[128,128,256]{2,1,0:T(8,128)(2,1)} %gather_fusion.1, bf16[128,128,128]{2,1,0:T(8,128)(2,1)} %param.9, f32[128]{0:T(128)S(1)} %convert_element_type.9), kind=kOutput, calls=%fused_computation.4 | convolution fusion | flops 1077936128 | bytes 29360640 | tf_op jit(solution)/shard_map/sab,saf->sbf/dot_general | solution.py:31
  226.0 0.0 copy-start.5
  226.0 17.5 %copy.14 = f32[128,128,256]{2,1,0:T(8,128)} copy(f32[128,128,256]{1,2,0:T(8,128)} %multiply_bitcast_fusion) | data formatting | bytes 33554432 | tf_op jit(solution)/shard_map/mul | solution.py:34
  243.5 0.0 copy-done.5
  243.5 0.0 copy-start.1
  243.5 24.0 %scatter_fusion.1 = f32[2,128,256]{2,1,0:T(8,128)S(1)} fusion(f32[2,128,256]{2,1,0:T(8,128)S(1)} %broadcast_in_dim.22, s32[128]{0:T(128)S(1)} %copy-done.5, f32[128,128,256]{2,1,0:T(8,128)} %copy.14), kind=kCustom, calls=%fused_computation.3 | custom fusion | flops 4194304 | bytes 50332160 | tf_op jit(solution)/shard_map/scatter-add | solution.py:35
  267.5 0.0 copy-start.2
  267.5 0.7 copy-done.2
  268.2 0.0 copy-done.1
  (5 shorter events, 0.0 us)
Async XLA Ops:
  6.5 1.4 copy-start
  6.5 154.0 %reduce-scatter.2.cloned.1.call-start = ((), (), s32[]{:S(2)}) async-start(), calls=%async_computation.1 | async-start | bytes 4456448 | tf_op jit(solution)/shard_map/reduce_scatter | solution.py:23
  27.2 17.5 %copy-start.6 = (s32[128]{0:T(128)S(1)}, s32[128]{0:T(128)}, u32[]{:S(2)}) copy-start(s32[128]{0:T(128)} %param.11) | copy-start | bytes 1540
  27.2 17.5 %copy-start.7 = (s32[128,1]{0,1:T(1,128)S(1)}, s32[128,1]{0,1:T(1,128)}, u32[]{:S(2)}) copy-start(s32[128,1]{0,1:T(1,128)} %param.10) | copy-start | bytes 1540
  47.1 114.5 %copy-start.3 = (bf16[256,256]{1,0:T(8,128)(2,1)S(1)}, bf16[256,256]{1,0:T(8,128)(2,1)}, u32[]{:S(2)}) copy-start(bf16[256,256]{1,0:T(8,128)(2,1)} %param.15) | copy-start | bytes 393220
  47.1 114.5 %copy-start.4 = (f32[256]{0:T(256)S(1)}, f32[256]{0:T(256)}, u32[]{:S(2)}) copy-start(f32[256]{0:T(256)} %param.14) | copy-start | bytes 3076
  85.0 119.2 %all-gather.2.cloned.1.call-start = ((), (), s32[]{:S(2)}) async-start(), calls=%async_computation.2 | async-start | bytes 2228224 | tf_op jit(solution)/shard_map/all_gather | solution.py:29
  226.0 17.5 %copy-start.5 = (s32[128]{0:T(128)S(1)}, s32[128]{0:T(128)}, u32[]{:S(2)}) copy-start(s32[128]{0:T(128)} %param.12) | copy-start | bytes 1540
  243.5 24.7 %copy-start.1 = (bf16[256,256]{1,0:T(8,128)(2,1)S(1)}, bf16[256,256]{1,0:T(8,128)(2,1)}, u32[]{:S(2)}) copy-start(bf16[256,256]{1,0:T(8,128)(2,1)} %param.8) | copy-start | bytes 393220
  267.5 0.7 copy-start.2
Sparse Core Ops, SparseCore 0:
  85.1 75.3 reduce-scatter.1
  163.6 40.5 all-gather.1
where the time goes:
time: 276 us; the launch traced here: 275 us
  waiting for transfers between devices  116 us (42%)
  other arithmetic  64.2 us (23%)
  local copies, waits for them, and re-layouts  52.7 us (19%)
  matrix products  28.4 us (10%)
  between operations  13.5 us (5%)
    reduce_scatter x1, waiting for transfers between devices, body(): lax.psum_scatter(partial_sums, 'col', scatter_dimension=0, tiled=True)  75.3 us
    all_gather x1, waiting for transfers between devices, body(): all_hidden = lax.all_gather(hidden, 'col', axis=0, tiled=True)  40.7 us
    scatter-add x1, other arithmetic, body(): jax.ops.segment_sum(products, row_block, num_segments=devices * per_dev)  37.8 us
    scatter-add x1, other arithmetic, body(): result_rows = jax.ops.segment_sum(returned, block_col, num_segments=per_dev)  24 us
    mul x1, local copies, waits for them, and re-layouts, body(): returned = returned * live_mask[:, None, None]  17.5 us
    mul x1, local copies, waits for them, and re-layouts, body(): products = products * live_mask[:, None, None]  17.5 us
    dot_general x1, matrix products, body(): jnp.einsum('sab,saf->sbf', block_values, picked_hidden, preferred_element...  13.7 us
    dot_general x1, matrix products, body(): jnp.einsum('sab,sbf->saf', block_values, source_rows, preferred_element_t...  12.9 us
  transfers between devices with their start and end apart: 2, of which 2 were waited for; matrix products, arithmetic and copies ran while one was open for 0% of the time, Pallas kernels for 0%

commit v1 on v0

v1 whole, which is shorter than its diff:
```python
import functools

import jax
import jax.numpy as jnp
from jax import lax
from jax.experimental import pallas as pl
from jax.experimental.pallas import tpu as pltpu
from jax.sharding import PartitionSpec as P

MIB = 1024 * 1024
CHUNKS = 8


def merge_kernel(n, bs, nb, owner_ref, sub_ref, col_ref, valid_ref, values_ref, hi_ref, lo_ref,
                 dense, staged, sems):
    zs = n // 4
    per = nb // CHUNKS

    def chunk(i):
        part = pl.ds(i * per, per)
        return pltpu.make_async_copy(values_ref.at[part], staged.at[part], sems.at[i])

    for i in range(CHUNKS):
        chunk(i).start()

    @pl.loop(0, n)
    def _(d):
        dense[d] = jnp.zeros(dense.shape[1:], jnp.float32)

    for i in range(CHUNKS):
        chunk(i).wait()

        @pl.loop(i * per, (i + 1) * per)
        def _(s):
            owner = owner_ref[s]
            place = (owner % 2 * 2 + owner // 2 % 2) * zs + owner // 4
            rows = pl.ds(pl.multiple_of(sub_ref[s] * bs, bs), bs)
            columns = pl.ds(pl.multiple_of(col_ref[s] * bs, bs), bs)
            live = valid_ref[s].astype(jnp.float32)
            dense[place, rows, columns] += staged[s].astype(jnp.float32) * live

    @pl.loop(0, n)
    def _(d):
        whole = dense[d]
        head = whole.astype(jnp.bfloat16)
        hi_ref[d] = head
        lo_ref[d] = (whole - head.astype(jnp.float32)).astype(jnp.bfloat16)


def layer_kernel(n, hi_ref, lo_ref, x_ref, gain_ref, w_ref, out_ref,
                 pa_send, pa_recv, yb_send, yb_recv, zb_send, zb_recv, acc, agg, hbuf, out_t,
                 pa_ss, pa_rs, yb_ss, yb_rs, zb_ss, zb_rs, hz_ss, hz_rs, hy_ss, hy_rs, hc_ss, hc_rs):
    zs = n // 4
    me = lax.axis_index("col")
    z, y, c = me // 4, me // 2 % 2, me % 2
    other_core = me + 1 - 2 * c
    other_y = me + 2 - 4 * y

    def dest(z_to):
        return z_to * 4 + y * 2 + c

    barrier = pltpu.get_barrier_semaphore()

    def greet(device):
        pl.semaphore_signal(barrier, inc=1, device_id={"col": device},
                            device_id_type=pl.DeviceIdType.MESH)

    greet(other_core)
    greet(other_y)
    for i in range(1, zs):
        greet(dest((z + i) % zs))
    pl.semaphore_wait(barrier, zs + 1)

    def remote(src, dst, ss, rs, device):
        return pltpu.make_async_remote_copy(
            src_ref=src, dst_ref=dst, send_sem=ss, recv_sem=rs,
            device_id={"col": device}, device_id_type=pl.DeviceIdType.MESH)

    def product(place):
        x = x_ref[...]
        return (jnp.dot(hi_ref[place], x, preferred_element_type=jnp.float32)
                + jnp.dot(lo_ref[place], x, preferred_element_type=jnp.float32))

    def core_copy(j):
        return remote(pa_send.at[j], pa_recv.at[j], pa_ss.at[j], pa_rs.at[j], other_core)

    def turned(k):
        return (k + (1 - y) * zs) % (2 * zs)

    @pl.loop(0, 2 * zs)
    def _(k):
        j = turned(k)
        pa_send[j] = product((1 - c) * 2 * zs + j)
        core_copy(j).start()

    @pl.loop(0, 2 * zs)
    def _(k):
        j = turned(k)
        acc[j] = product(c * 2 * zs + j)

    def y_copy(k):
        return remote(yb_send.at[k], yb_recv.at[k], yb_ss.at[k], yb_rs.at[k], other_y)

    @pl.loop(0, zs)
    def _(k):
        k = (z + 1 + k) % zs
        j = (1 - y) * zs + k
        core_copy(j).wait_recv()
        yb_send[k] = (acc[j] + pa_recv[j]).astype(jnp.bfloat16)
        y_copy(k).start()

    @pl.loop(0, zs)
    def _(k):
        j = y * zs + k
        core_copy(j).wait_recv()
        acc[j] = acc[j] + pa_recv[j]

    def z_copy(i):
        return remote(zb_send.at[i], zb_recv.at[i], zb_ss.at[i], zb_rs.at[i], dest((z + i) % zs))

    @pl.loop(1, zs)
    def _(i):
        k = (z + i) % zs
        y_copy(k).wait_recv()
        zb_send[i] = (acc[y * zs + k] + yb_recv[k].astype(jnp.float32)).astype(jnp.bfloat16)
        z_copy(i).start()

    y_copy(z).wait_recv()
    agg[...] = acc[y * zs + z] + yb_recv[z].astype(jnp.float32)

    @pl.loop(1, zs)
    def _(i):
        z_copy(i).wait_recv()
        agg[...] += zb_recv[i].astype(jnp.float32)

    total = agg[...]
    scale = lax.rsqrt(jnp.mean(total * total, axis=1, keepdims=True) + 1e-06)
    normed = (total * scale * gain_ref[...]).astype(jnp.bfloat16)
    hidden = jnp.maximum(jnp.dot(normed, w_ref[...], preferred_element_type=jnp.float32), 0.0)
    mine = (c * 2 + y) * zs + z
    hbuf[mine] = hidden.T.astype(jnp.bfloat16)

    def hz_copy(i):
        return remote(hbuf.at[mine], hbuf.at[mine], hz_ss.at[i], hz_rs.at[i], dest((z + i) % zs))

    def hz_wait(i):
        slot = (c * 2 + y) * zs + (z - i + zs) % zs
        remote(hbuf.at[slot], hbuf.at[slot], hz_ss.at[i], hz_rs.at[i], other_y).wait_recv()
        return slot

    def hy_copy(i, y_of):
        slot = (c * 2 + y_of) * zs + (z - i + zs) % zs
        return slot, remote(hbuf.at[slot], hbuf.at[slot], hy_ss.at[i], hy_rs.at[i], other_y)

    def hc_copy(i, c_of, y_of):
        slot = (c_of * 2 + y_of) * zs + (z - i + zs) % zs
        k = (y_of + y) % 2 * zs + i
        return slot, remote(hbuf.at[slot], hbuf.at[slot], hc_ss.at[k], hc_rs.at[k], other_core)

    for i in range(1, zs):
        hz_copy(i).start()

    hy_copy(0, y)[1].start()
    hc_copy(0, c, y)[1].start()
    out_t[...] = jnp.zeros(out_t.shape, jnp.float32)

    def take(slot):
        out_t[...] += (jnp.dot(hbuf[slot], hi_ref[slot], preferred_element_type=jnp.float32)
                       + jnp.dot(hbuf[slot], lo_ref[slot], preferred_element_type=jnp.float32))

    take(mine)

    @pl.loop(1, zs)
    def _(i):
        slot = hz_wait(i)
        hy_copy(i, y)[1].start()
        hc_copy(i, c, y)[1].start()
        take(slot)

    @pl.loop(0, zs)
    def _(i):
        slot, copy = hy_copy(i, 1 - y)
        copy.wait_recv()
        hc_copy(i, c, 1 - y)[1].start()
        take(slot)

    @pl.loop(0, 2 * zs)
    def _(k):
        slot, copy = hc_copy(k % zs, 1 - c, (k // zs + y) % 2)
        copy.wait_recv()
        take(slot)

    out_ref[...] = out_t[...].T

    @pl.loop(0, 2 * zs)
    def _(j):
        core_copy(j).wait_send()

    @pl.loop(0, zs)
    def _(k):
        y_copy(k).wait_send()

    @pl.loop(1, zs)
    def _(i):
        z_copy(i).wait_send()
        hz_copy(i).wait_send()

    @pl.loop(0, zs)
    def _(i):
        hy_copy(i, y)[1].wait_send()
        hc_copy(i, c, y)[1].wait_send()
        hc_copy(i, c, 1 - y)[1].wait_send()


def solution(mesh):
    n = mesh.shape["col"]
    zs = n // 4

    def body(features, block_values, block_owner, block_sub, block_col, block_valid, norm_gain,
             weight):
        nb, bs = block_values.shape[:2]
        rows, width = features.shape
        smem = pl.BlockSpec(memory_space=pltpu.SMEM)
        vmem = pl.BlockSpec(memory_space=pltpu.VMEM)
        blocks = jax.ShapeDtypeStruct((n, rows, rows), jnp.bfloat16)
        hi, lo = pl.pallas_call(
            functools.partial(merge_kernel, n, bs, nb),
            out_shape=(blocks, blocks),
            in_specs=[smem] * 4 + [pl.BlockSpec(memory_space=pl.ANY)],
            out_specs=(vmem, vmem),
            scratch_shapes=[
                pltpu.VMEM((n, rows, rows), jnp.float32),
                pltpu.VMEM((nb, bs, bs), jnp.bfloat16),
                pltpu.SemaphoreType.DMA((CHUNKS,)),
            ],
            compiler_params=pltpu.CompilerParams(vmem_limit_bytes=44 * MIB),
        )(block_owner[:, 0], block_sub, block_col, block_valid, block_values)

        f32, bf16 = jnp.float32, jnp.bfloat16
        dma = pltpu.SemaphoreType.DMA
        return pl.pallas_call(
            functools.partial(layer_kernel, n),
            out_shape=jax.ShapeDtypeStruct((rows, width), f32),
            in_specs=[vmem] * 5,
            out_specs=vmem,
            scratch_shapes=[
                pltpu.VMEM((2 * zs, rows, width), f32),
                pltpu.VMEM((2 * zs, rows, width), f32),
                pltpu.VMEM((zs, rows, width), bf16),
                pltpu.VMEM((zs, rows, width), bf16),
                pltpu.VMEM((zs, rows, width), bf16),
                pltpu.VMEM((zs, rows, width), bf16),
                pltpu.VMEM((2 * zs, rows, width), f32),
                pltpu.VMEM((rows, width), f32),
                pltpu.VMEM((n, width, rows), bf16),
                pltpu.VMEM((width, rows), f32),
                dma((2 * zs,)), dma((2 * zs,)), dma((zs,)), dma((zs,)), dma((zs,)), dma((zs,)),
                dma((zs,)), dma((zs,)), dma((zs,)), dma((zs,)), dma((2 * zs,)), dma((2 * zs,)),
            ],
            compiler_params=pltpu.CompilerParams(
                collective_id=0, has_side_effects=True, vmem_limit_bytes=60 * MIB),
        )(hi, lo, features, norm_gain[None, :], weight)

    placed = (
        P(("groups", "col"), None),
        P(("groups", "col"), None, None),
        P(("groups", "col"), None),
        P(("groups", "col")),
        P(("groups", "col")),
        P(("groups", "col")),
        P(),
        P(),
    )
    return jax.shard_map(
        body, mesh=mesh, in_specs=placed, out_specs=P(("groups", "col"), None), check_vma=False
    )
```

time: 276 us -> 63.6 us (0.23)
  the two profiles are of different devices: /device:TPU:0 before, /device:TPU:20 now
where the time goes in v1:
time: 63.6 us; the launch traced here: 63.4 us
  Pallas kernels  54.2 us (85%)
  local copies, waits for them, and re-layouts  9.13 us (14%)
    pallas_call x1, Pallas kernels, body(): pl.pallas_call(functools.partial(layer_kernel, n), out_shape=jax.ShapeDty...  49.2 us
    unnamed x15, local copies, waits for them, and re-layouts  9.13 us
    pallas_call x1, Pallas kernels, body(): pl.pallas_call(functools.partial(merge_kernel, n, bs, nb), out_shape=(blo...  5.04 us

profile of v1, /device:TPU:20, one launch (start us, length us, event | category | flops | bytes accessed | tf_op | source)
XLA Modules:
  0.0 63.4 jit_solution(8742834464339745448)
XLA Ops:
  0.0 0.0 copy-start
  0.0 2.2 %copy-done = bf16[128,128,128]{2,1,0:T(8,128)(2,1)S(1)} copy-done((bf16[128,128,128]{2,1,0:T(8,128)(2,1)S(1)}, bf16[128,128,128]{2,1,0:T(8,128)(2,1)}, u32[]{:S(2)}) %copy-start) | copy-done | bytes 4194328
  2.2 0.0 copy-start.3
  2.2 0.7 %copy-done.3 = s32[128,1]{0,1:T(1,128)S(1)} copy-done((s32[128,1]{0,1:T(1,128)S(1)}, s32[128,1]{0,1:T(1,128)}, u32[]{:S(2)}) %copy-start.3) | copy-done | bytes 536
  2.8 0.0 copy-start.4
  2.8 0.7 %copy-done.4 = s32[128]{0:T(128)S(1)} copy-done((s32[128]{0:T(128)S(1)}, s32[128]{0:T(128)}, u32[]{:S(2)}) %copy-start.4) | copy-done | bytes 536
  3.5 0.0 copy-start.5
  3.5 0.7 %copy-done.5 = s32[128]{0:T(128)S(1)} copy-done((s32[128]{0:T(128)S(1)}, s32[128]{0:T(128)}, u32[]{:S(2)}) %copy-start.5) | copy-done | bytes 536
  4.2 0.0 copy-start.6
  4.2 0.7 %copy-done.6 = s32[128]{0:T(128)S(1)} copy-done((s32[128]{0:T(128)S(1)}, s32[128]{0:T(128)}, u32[]{:S(2)}) %copy-start.6) | copy-done | bytes 536
  4.8 5.0 %shard_map.82 = (bf16[16,256,256]{2,1,0:T(8,128)(2,1)S(1)}, bf16[16,256,256]{2,1,0:T(8,128)(2,1)S(1)}) custom-call(s32[128]{0:T(128)S(1)} %bitcast.2, s32[128]{0:T(128)S(1)} %copy-done.4, s32[128]{0:T(128)S(1)} %copy-done.5, s32[128]{0:T(128)S(1)} %copy-done.6, bf16[128,128,128]{2,1,0:T(8,128)(2,1)S(1)} %copy-done), custom_call_target="tpu_custom_call" | custom-call | tf_op jit(solution)/shard_map/pallas_call | solution.py:226
  9.9 0.0 copy-start.1
  9.9 1.3 %copy-done.1 = bf16[16,256,256]{2,1,0:T(8,128)(2,1)} copy-done((bf16[16,256,256]{2,1,0:T(8,128)(2,1)}, bf16[16,256,256]{2,1,0:T(8,128)(2,1)S(1)}, u32[]{:S(2)}) %copy-start.1) | copy-done | bytes 2097176
  11.2 0.0 copy-start.2
  11.2 1.3 %copy-done.2 = bf16[16,256,256]{2,1,0:T(8,128)(2,1)} copy-done((bf16[16,256,256]{2,1,0:T(8,128)(2,1)}, bf16[16,256,256]{2,1,0:T(8,128)(2,1)S(1)}, u32[]{:S(2)}) %copy-start.2) | copy-done | bytes 2097176
  12.5 49.2 %shard_map.83 = f32[256,256]{1,0:T(8,128)} custom-call(bf16[16,256,256]{2,1,0:T(8,128)(2,1)} %copy-done.1, bf16[16,256,256]{2,1,0:T(8,128)(2,1)} %copy-done.2, bf16[256,256]{1,0:T(8,128)(2,1)} %x_ref.1, f32[1,256]{1,0:T(1,128)} %bitcast.3, bf16[256,256]{1,0:T(8,128)(2,1)} %w_ref.1), custom_call_target="tpu_custom_call" | custom-call | tf_op jit(solution)/shard_map/pallas_call | solution.py:241
  61.7 1.7 %copy.10 = f32[256,256]{1,0:T(8,128)} copy(f32[256,256]{1,0:T(8,128)} %shard_map.83) | data formatting | bytes 524288
Async XLA Ops:
  0.0 2.2 %copy-start = (bf16[128,128,128]{2,1,0:T(8,128)(2,1)S(1)}, bf16[128,128,128]{2,1,0:T(8,128)(2,1)}, u32[]{:S(2)}) copy-start(bf16[128,128,128]{2,1,0:T(8,128)(2,1)} %values_ref.1) | copy-start | bytes 12582916
  2.2 0.7 %copy-start.3 = (s32[128,1]{0,1:T(1,128)S(1)}, s32[128,1]{0,1:T(1,128)}, u32[]{:S(2)}) copy-start(s32[128,1]{0,1:T(1,128)} %param.10) | copy-start | bytes 1540
  2.8 0.7 %copy-start.4 = (s32[128]{0:T(128)S(1)}, s32[128]{0:T(128)}, u32[]{:S(2)}) copy-start(s32[128]{0:T(128)} %sub_ref.1) | copy-start | bytes 1540
  3.5 0.7 %copy-start.5 = (s32[128]{0:T(128)S(1)}, s32[128]{0:T(128)}, u32[]{:S(2)}) copy-start(s32[128]{0:T(128)} %col_ref.1) | copy-start | bytes 1540
  4.2 0.7 %copy-start.6 = (s32[128]{0:T(128)S(1)}, s32[128]{0:T(128)}, u32[]{:S(2)}) copy-start(s32[128]{0:T(128)} %valid_ref.1) | copy-start | bytes 1540
  9.9 1.3 %copy-start.1 = (bf16[16,256,256]{2,1,0:T(8,128)(2,1)}, bf16[16,256,256]{2,1,0:T(8,128)(2,1)S(1)}, u32[]{:S(2)}) copy-start(bf16[16,256,256]{2,1,0:T(8,128)(2,1)S(1)} %get-tuple-element.7.hi_ref) | copy-start | bytes 6291460
  11.2 1.3 %copy-start.2 = (bf16[16,256,256]{2,1,0:T(8,128)(2,1)}, bf16[16,256,256]{2,1,0:T(8,128)(2,1)S(1)}, u32[]{:S(2)}) copy-start(bf16[16,256,256]{2,1,0:T(8,128)(2,1)S(1)} %get-tuple-element.8.lo_ref) | copy-start | bytes 6291460

commit v2 on v1

--- a/solution.py
+++ b/solution.py
@@ -11,8 +11,8 @@
 CHUNKS = 8
 
 
-def merge_kernel(n, bs, nb, owner_ref, sub_ref, col_ref, valid_ref, values_ref, hi_ref, lo_ref,
-                 dense, staged, sems):
+def merge_kernel(n, bs, nb, owner_hbm, sub_hbm, col_hbm, valid_hbm, values_ref, hi_ref, lo_ref,
+                 dense, staged, owner_ref, sub_ref, col_ref, valid_ref, sems, index_sems):
     zs = n // 4
     per = nb // CHUNKS
 
@@ -20,12 +20,22 @@
         part = pl.ds(i * per, per)
         return pltpu.make_async_copy(values_ref.at[part], staged.at[part], sems.at[i])
 
+    indices = [
+        pltpu.make_async_copy(src, dst, index_sems.at[i])
+        for i, (src, dst) in enumerate((
+            (owner_hbm, owner_ref), (sub_hbm, sub_ref), (col_hbm, col_ref), (valid_hbm, valid_ref)))
+    ]
+    for copy in indices:
+        copy.start()
     for i in range(CHUNKS):
         chunk(i).start()
 
     @pl.loop(0, n)
     def _(d):
         dense[d] = jnp.zeros(dense.shape[1:], jnp.float32)
+
+    for copy in indices:
+        copy.wait()
 
     for i in range(CHUNKS):
         chunk(i).wait()
@@ -47,7 +57,7 @@
         lo_ref[d] = (whole - head.astype(jnp.float32)).astype(jnp.bfloat16)
 
 
-def layer_kernel(n, hi_ref, lo_ref, x_ref, gain_ref, w_ref, out_ref,
+def layer_kernel(n, cut, hi_ref, lo_ref, x_ref, gain_ref, w_ref, out_ref,
                  pa_send, pa_recv, yb_send, yb_recv, zb_send, zb_recv, acc, agg, hbuf, out_t,
                  pa_ss, pa_rs, yb_ss, yb_rs, zb_ss, zb_rs, hz_ss, hz_rs, hy_ss, hy_rs, hc_ss, hc_rs):
     zs = n // 4
@@ -140,57 +150,114 @@
     mine = (c * 2 + y) * zs + z
     hbuf[mine] = hidden.T.astype(jnp.bfloat16)
 
-    def hz_copy(i):
-        return remote(hbuf.at[mine], hbuf.at[mine], hz_ss.at[i], hz_rs.at[i], dest((z + i) % zs))
-
-    def hz_wait(i):
-        slot = (c * 2 + y) * zs + (z - i + zs) % zs
-        remote(hbuf.at[slot], hbuf.at[slot], hz_ss.at[i], hz_rs.at[i], other_y).wait_recv()
-        return slot
-
-    def hy_copy(i, y_of):
-        slot = (c * 2 + y_of) * zs + (z - i + zs) % zs
-        return slot, remote(hbuf.at[slot], hbuf.at[slot], hy_ss.at[i], hy_rs.at[i], other_y)
-
-    def hc_copy(i, c_of, y_of):
-        slot = (c_of * 2 + y_of) * zs + (z - i + zs) % zs
-        k = (y_of + y) % 2 * zs + i
-        return slot, remote(hbuf.at[slot], hbuf.at[slot], hc_ss.at[k], hc_rs.at[k], other_core)
-
-    for i in range(1, zs):
-        hz_copy(i).start()
-
-    hy_copy(0, y)[1].start()
-    hc_copy(0, c, y)[1].start()
+    parts = (pl.ds(0, cut), pl.ds(cut, hbuf.shape[1] - cut))
+
+    def slot_of(c_of, y_of, z_of):
+        return (c_of * 2 + y_of) * zs + z_of
+
+    STREAMS = ((0, y), (1, y), (1, 1 - y))
+
+    def chain(stream, z_of, way):
+        part, y_of = STREAMS[stream]
+        ref = hbuf.at[slot_of(c, y_of, z_of), parts[part]]
+        return remote(ref, ref, hz_ss.at[way * 3 * zs + stream * zs + z_of],
+                      hz_rs.at[stream * zs + z_of], dest((z + 1 - 2 * way + zs) % zs))
+
+    def across(part, y_of, z_of):
+        ref = hbuf.at[slot_of(c, y_of, z_of), parts[part]]
+        k = z_of if part == 0 else zs
+        return remote(ref, ref, hy_ss.at[k], hy_rs.at[k], other_y)
+
+    def pair(part, c_of, y_of, z_of):
+        slot = slot_of(c_of, y_of, z_of)
+        ref = hbuf.at[slot, parts[part]]
+        k = part * 2 * zs + y_of * zs + z_of
+        return remote(ref, ref, hc_ss.at[k], hc_rs.at[k], other_core)
+
     out_t[...] = jnp.zeros(out_t.shape, jnp.float32)
 
     def take(slot):
         out_t[...] += (jnp.dot(hbuf[slot], hi_ref[slot], preferred_element_type=jnp.float32)
                        + jnp.dot(hbuf[slot], lo_ref[slot], preferred_element_type=jnp.float32))
 
+    def can_go(way):
+        return z + 1 < zs if way == 0 else z > 0
+
+    def take_other(z_of):
+        for y_of in (y, 1 - y):
+            for part in (0, 1):
+                pair(part, 1 - c, y_of, z_of).wait_recv()
+            take(slot_of(1 - c, y_of, z_of))
+
+    across(1, y, z).start()
+    for way in (0, 1):
+        @pl.when(can_go(way))
+        def _():
+            chain(0, z, way).start()
+            chain(1, z, way).start()
+    across(0, y, z).start()
+    pair(0, c, y, z).start()
+    pair(1, c, y, z).start()
+    across(1, 1 - y, z).wait_recv()
+    for way in (0, 1):
+        @pl.when(can_go(way))
+        def _():
+            chain(2, z, way).start()
+    pair(1, c, 1 - y, z).start()
     take(mine)
+    across(0, 1 - y, z).wait_recv()
+    pair(0, c, 1 - y, z).start()
+    take(slot_of(c, 1 - y, z))
+
+    def has(way, i):
+        return z - i >= 0 if way == 0 else z + i < zs
+
+    def came(way, i):
+        return z - i if way == 0 else z + i
+
+    def both_ways(i, do):
+        for way in (0, 1):
+            @pl.when(has(way, i))
+            def _():
+                do(way, came(way, i))
 
     @pl.loop(1, zs)
     def _(i):
-        slot = hz_wait(i)
-        hy_copy(i, y)[1].start()
-        hc_copy(i, c, y)[1].start()
-        take(slot)
-
-    @pl.loop(0, zs)
-    def _(i):
-        slot, copy = hy_copy(i, 1 - y)
-        copy.wait_recv()
-        hc_copy(i, c, 1 - y)[1].start()
-        take(slot)
-
-    @pl.loop(0, 2 * zs)
-    def _(k):
-        slot, copy = hc_copy(k % zs, 1 - c, (k // zs + y) % 2)
-        copy.wait_recv()
-        take(slot)
-
-    out_ref[...] = out_t[...].T
+        for stream in (0, 1, 2):
+            def arrive(way, z_of):
+                chain(stream, z_of, way).wait_recv()
+
+                @pl.when(can_go(way))
+                def _():
+                    chain(stream, z_of, way).start()
+
+                part, y_of = STREAMS[stream]
+                if stream == 0:
+                    across(0, y, z_of).start()
+                pair(part, c, y_of, z_of).start()
+
+            both_ways(i, arrive)
+
+        both_ways(i, lambda way, z_of: take(slot_of(c, y, z_of)))
+
+        def far(way, z_of):
+            across(0, 1 - y, z_of).wait_recv()
+            pair(0, c, 1 - y, z_of).start()
+            take(slot_of(c, 1 - y, z_of))
+
+        both_ways(i, far)
+
+        @pl.when(i == 1)
+        def _():
+            take_other(z)
+
+        @pl.when(i > 1)
+        def _():
+            both_ways(i - 1, lambda way, z_of: take_other(z_of))
+
+    both_ways(zs - 1, lambda way, z_of: take_other(z_of))
+
+    out_ref[...] = out_t[...]
 
     @pl.loop(0, 2 * zs)
     def _(j):
@@ -203,13 +270,22 @@
     @pl.loop(1, zs)
     def _(i):
         z_copy(i).wait_send()
-        hz_copy(i).wait_send()
+
+    across(1, y, z).wait_send()
 
     @pl.loop(0, zs)
-    def _(i):
-        hy_copy(i, y)[1].wait_send()
-        hc_copy(i, c, y)[1].wait_send()
-        hc_copy(i, c, 1 - y)[1].wait_send()
+    def _(k):
+        across(0, y, k).wait_send()
+        for y_of in (0, 1):
+            for part in (0, 1):
+                pair(part, c, y_of, k).wait_send()
+        for way in (0, 1):
+            from_there = k <= z if way == 0 else k >= z
+
+            @pl.when(can_go(way) & from_there)
+            def _():
+                for stream in (0, 1, 2):
+                    chain(stream, k, way).wait_send()
 
 
 def solution(mesh):
@@ -220,27 +296,30 @@
              weight):
         nb, bs = block_values.shape[:2]
         rows, width = features.shape
-        smem = pl.BlockSpec(memory_space=pltpu.SMEM)
+        hbm = pl.BlockSpec(memory_space=pltpu.HBM)
+        vmem_limit = (n + 6) * 7 // 8 * MIB
         vmem = pl.BlockSpec(memory_space=pltpu.VMEM)
         blocks = jax.ShapeDtypeStruct((n, rows, rows), jnp.bfloat16)
         hi, lo = pl.pallas_call(
             functools.partial(merge_kernel, n, bs, nb),
             out_shape=(blocks, blocks),
-            in_specs=[smem] * 4 + [pl.BlockSpec(memory_space=pl.ANY)],
+            in_specs=[hbm] * 5,
             out_specs=(vmem, vmem),
             scratch_shapes=[
                 pltpu.VMEM((n, rows, rows), jnp.float32),
                 pltpu.VMEM((nb, bs, bs), jnp.bfloat16),
+            ] + [pltpu.SMEM((nb,), jnp.int32)] * 4 + [
                 pltpu.SemaphoreType.DMA((CHUNKS,)),
+                pltpu.SemaphoreType.DMA((4,)),
             ],
-            compiler_params=pltpu.CompilerParams(vmem_limit_bytes=44 * MIB),
+            compiler_params=pltpu.CompilerParams(vmem_limit_bytes=vmem_limit),
         )(block_owner[:, 0], block_sub, block_col, block_valid, block_values)
 
         f32, bf16 = jnp.float32, jnp.bfloat16
         dma = pltpu.SemaphoreType.DMA
         return pl.pallas_call(
-            functools.partial(layer_kernel, n),
-            out_shape=jax.ShapeDtypeStruct((rows, width), f32),
+            functools.partial(layer_kernel, n, width * 5 // 8),
+            out_shape=jax.ShapeDtypeStruct((width, rows), f32),
             in_specs=[vmem] * 5,
             out_specs=vmem,
             scratch_shapes=[
@@ -255,11 +334,12 @@
                 pltpu.VMEM((n, width, rows), bf16),
                 pltpu.VMEM((width, rows), f32),
                 dma((2 * zs,)), dma((2 * zs,)), dma((zs,)), dma((zs,)), dma((zs,)), dma((zs,)),
-                dma((zs,)), dma((zs,)), dma((zs,)), dma((zs,)), dma((2 * zs,)), dma((2 * zs,)),
+                dma((6 * zs,)), dma((3 * zs,)), dma((zs + 1,)), dma((zs + 1,)),
+                dma((4 * zs,)), dma((4 * zs,)),
             ],
             compiler_params=pltpu.CompilerParams(
-                collective_id=0, has_side_effects=True, vmem_limit_bytes=60 * MIB),
-        )(hi, lo, features, norm_gain[None, :], weight)
+                collective_id=0, has_side_effects=True, vmem_limit_bytes=vmem_limit),
+        )(hi, lo, features, norm_gain[None, :], weight).T
 
     placed = (
         P(("groups", "col"), None),

time: 63.6 us -> 56.5 us (0.89)
  the two profiles are of different devices: /device:TPU:20 before, /device:TPU:0 now
where the time goes in v2:
time: 56.5 us; the launch traced here: 56.3 us
  Pallas kernels  50.6 us (90%)
  local copies, waits for them, and re-layouts  5.65 us (10%)
    pallas_call x1, Pallas kernels, body(): pl.pallas_call(functools.partial(layer_kernel, n, width * 5 // 8), out_sh...  46 us
    unnamed x16, local copies, waits for them, and re-layouts  4.82 us
    pallas_call x1, Pallas kernels, body(): pl.pallas_call(functools.partial(merge_kernel, n, bs, nb), out_shape=(blo...  4.55 us

profile of v2, /device:TPU:0, one launch (start us, length us, event | category | flops | bytes accessed | tf_op | source)
XLA Modules:
  0.0 56.3 jit_solution(7379618524957374521)
XLA Ops:
  0.0 0.0 copy-start
  0.0 2.2 %copy-done = bf16[128,128,128]{2,1,0:T(8,128)(2,1)S(1)} copy-done((bf16[128,128,128]{2,1,0:T(8,128)(2,1)S(1)}, bf16[128,128,128]{2,1,0:T(8,128)(2,1)}, u32[]{:S(2)}) %copy-start) | copy-done | bytes 4194328
  2.2 0.0 copy-start.4
  2.2 0.7 %copy-done.4 = s32[128,1]{0,1:T(1,128)S(1)} copy-done((s32[128,1]{0,1:T(1,128)S(1)}, s32[128,1]{0,1:T(1,128)}, u32[]{:S(2)}) %copy-start.4) | copy-done | bytes 536
  2.8 0.0 copy-start.5
  2.8 0.7 %copy-done.5 = s32[128]{0:T(128)S(1)} copy-done((s32[128]{0:T(128)S(1)}, s32[128]{0:T(128)}, u32[]{:S(2)}) %copy-start.5) | copy-done | bytes 536
  3.5 0.0 copy-start.6
  3.5 0.7 %copy-done.6 = s32[128]{0:T(128)S(1)} copy-done((s32[128]{0:T(128)S(1)}, s32[128]{0:T(128)}, u32[]{:S(2)}) %copy-start.6) | copy-done | bytes 536
  4.2 0.0 copy-start.7
  4.2 0.7 %copy-done.7 = s32[128]{0:T(128)S(1)} copy-done((s32[128]{0:T(128)S(1)}, s32[128]{0:T(128)}, u32[]{:S(2)}) %copy-start.7) | copy-done | bytes 536
  4.8 0.0 copy-start.1
  4.8 0.0 copy-start.2
  4.8 0.0 copy-start.3
  4.8 4.6 %shard_map.82 = (bf16[16,256,256]{2,1,0:T(8,128)(2,1)S(1)}, bf16[16,256,256]{2,1,0:T(8,128)(2,1)S(1)}) custom-call(s32[128]{0:T(128)S(1)} %bitcast.5, s32[128]{0:T(128)S(1)} %copy-done.5, s32[128]{0:T(128)S(1)} %copy-done.6, s32[128]{0:T(128)S(1)} %copy-done.7, bf16[128,128,128]{2,1,0:T(8,128)(2,1)S(1)} %copy-done), custom_call_target="tpu_custom_call" | custom-call | tf_op jit(solution)/shard_map/pallas_call | solution.py:303
  9.4 0.0 copy-done.1
  9.4 0.0 copy-done.2
  9.4 0.0 copy-done.3
  9.4 46.0 %shard_map.83 = f32[256,256]{1,0:T(8,128)S(1)} custom-call(bf16[16,256,256]{2,1,0:T(8,128)(2,1)S(1)} %get-tuple-element.7.hi_ref, bf16[16,256,256]{2,1,0:T(8,128)(2,1)S(1)} %get-tuple-element.8.lo_ref, bf16[256,256]{1,0:T(8,128)(2,1)S(1)} %copy-done.1, f32[1,256]{1,0:T(1,128)S(1)} %bitcast.4, bf16[256,256]{1,0:T(8,128)(2,1)S(1)} %copy-done.2), custom_call_target="tpu_custom_call" | custom-call | tf_op jit(solution)/shard_map/pallas_call | solution.py:320
  55.4 0.8 %copy.9 = f32[256,256]{1,0:T(8,128)} copy(f32[256,256]{0,1:T(8,128)S(1)} %bitcast.3) | data formatting | bytes 524288 | tf_op jit(solution)/shard_map/transpose | solution.py:342
Async XLA Ops:
  0.0 2.2 %copy-start = (bf16[128,128,128]{2,1,0:T(8,128)(2,1)S(1)}, bf16[128,128,128]{2,1,0:T(8,128)(2,1)}, u32[]{:S(2)}) copy-start(bf16[128,128,128]{2,1,0:T(8,128)(2,1)} %values_ref.1) | copy-start | bytes 12582916
  2.2 0.7 %copy-start.4 = (s32[128,1]{0,1:T(1,128)S(1)}, s32[128,1]{0,1:T(1,128)}, u32[]{:S(2)}) copy-start(s32[128,1]{0,1:T(1,128)} %param.10) | copy-start | bytes 1540
  2.8 0.7 %copy-start.5 = (s32[128]{0:T(128)S(1)}, s32[128]{0:T(128)}, u32[]{:S(2)}) copy-start(s32[128]{0:T(128)} %sub_hbm.1) | copy-start | bytes 1540
  3.5 0.7 %copy-start.6 = (s32[128]{0:T(128)S(1)}, s32[128]{0:T(128)}, u32[]{:S(2)}) copy-start(s32[128]{0:T(128)} %col_hbm.1) | copy-start | bytes 1540
  4.2 0.7 %copy-start.7 = (s32[128]{0:T(128)S(1)}, s32[128]{0:T(128)}, u32[]{:S(2)}) copy-start(s32[128]{0:T(128)} %valid_hbm.1) | copy-start | bytes 1540
  4.8 4.6 %copy-start.1 = (bf16[256,256]{1,0:T(8,128)(2,1)S(1)}, bf16[256,256]{1,0:T(8,128)(2,1)}, u32[]{:S(2)}) copy-start(bf16[256,256]{1,0:T(8,128)(2,1)} %x_ref.1) | copy-start | bytes 393220
  4.8 4.6 %copy-start.2 = (bf16[256,256]{1,0:T(8,128)(2,1)S(1)}, bf16[256,256]{1,0:T(8,128)(2,1)}, u32[]{:S(2)}) copy-start(bf16[256,256]{1,0:T(8,128)(2,1)} %w_ref.1) | copy-start | bytes 393220
  4.8 4.6 %copy-start.3 = (f32[256]{0:T(256)S(1)}, f32[256]{0:T(256)}, u32[]{:S(2)}) copy-start(f32[256]{0:T(256)} %param.14) | copy-start | bytes 3076

commit v3 on v1

--- a/solution.py
+++ b/solution.py
@@ -9,17 +9,20 @@
 
 MIB = 1024 * 1024
 CHUNKS = 8
-
-
-def merge_kernel(n, bs, nb, owner_ref, sub_ref, col_ref, valid_ref, values_ref, hi_ref, lo_ref,
-                 dense, staged, sems):
-    zs = n // 4
+CUTS = (7, 6, 3)
+
+
+def merge_kernel(bs, nb, index_any, values_ref, hi_ref, lo_ref, dense, staged, index_ref, sems,
+                 index_sem):
+    n = dense.shape[0]
     per = nb // CHUNKS
 
     def chunk(i):
         part = pl.ds(i * per, per)
         return pltpu.make_async_copy(values_ref.at[part], staged.at[part], sems.at[i])
 
+    index_copy = pltpu.make_async_copy(index_any, index_ref, index_sem)
+    index_copy.start()
     for i in range(CHUNKS):
         chunk(i).start()
 
@@ -27,16 +30,18 @@
     def _(d):
         dense[d] = jnp.zeros(dense.shape[1:], jnp.float32)
 
+    index_copy.wait()
+
     for i in range(CHUNKS):
         chunk(i).wait()
 
         @pl.loop(i * per, (i + 1) * per)
         def _(s):
-            owner = owner_ref[s]
-            place = (owner % 2 * 2 + owner // 2 % 2) * zs + owner // 4
-            rows = pl.ds(pl.multiple_of(sub_ref[s] * bs, bs), bs)
-            columns = pl.ds(pl.multiple_of(col_ref[s] * bs, bs), bs)
-            live = valid_ref[s].astype(jnp.float32)
+            index = index_ref[s]
+            place = index // 8
+            rows = pl.ds(pl.multiple_of(index // 4 % 2 * bs, bs), bs)
+            columns = pl.ds(pl.multiple_of(index // 2 % 2 * bs, bs), bs)
+            live = (index % 2).astype(jnp.float32)
             dense[place, rows, columns] += staged[s].astype(jnp.float32) * live
 
     @pl.loop(0, n)
@@ -47,7 +52,7 @@
         lo_ref[d] = (whole - head.astype(jnp.float32)).astype(jnp.bfloat16)
 
 
-def layer_kernel(n, hi_ref, lo_ref, x_ref, gain_ref, w_ref, out_ref,
+def layer_kernel(n, cuts, hi_ref, lo_ref, x_ref, gain_ref, w_ref, out_ref,
                  pa_send, pa_recv, yb_send, yb_recv, zb_send, zb_recv, acc, agg, hbuf, out_t,
                  pa_ss, pa_rs, yb_ss, yb_rs, zb_ss, zb_rs, hz_ss, hz_rs, hy_ss, hy_rs, hc_ss, hc_rs):
     zs = n // 4
@@ -69,7 +74,6 @@
     greet(other_y)
     for i in range(1, zs):
         greet(dest((z + i) % zs))
-    pl.semaphore_wait(barrier, zs + 1)
 
     def remote(src, dst, ss, rs, device):
         return pltpu.make_async_remote_copy(
@@ -91,7 +95,12 @@
     def _(k):
         j = turned(k)
         pa_send[j] = product((1 - c) * 2 * zs + j)
-        core_copy(j).start()
+
+    pl.semaphore_wait(barrier, zs + 1)
+
+    @pl.loop(0, 2 * zs)
+    def _(k):
+        core_copy(turned(k)).start()
 
     @pl.loop(0, 2 * zs)
     def _(k):
@@ -140,57 +149,97 @@
     mine = (c * 2 + y) * zs + z
     hbuf[mine] = hidden.T.astype(jnp.bfloat16)
 
-    def hz_copy(i):
-        return remote(hbuf.at[mine], hbuf.at[mine], hz_ss.at[i], hz_rs.at[i], dest((z + i) % zs))
-
-    def hz_wait(i):
-        slot = (c * 2 + y) * zs + (z - i + zs) % zs
-        remote(hbuf.at[slot], hbuf.at[slot], hz_ss.at[i], hz_rs.at[i], other_y).wait_recv()
-        return slot
-
-    def hy_copy(i, y_of):
-        slot = (c * 2 + y_of) * zs + (z - i + zs) % zs
-        return slot, remote(hbuf.at[slot], hbuf.at[slot], hy_ss.at[i], hy_rs.at[i], other_y)
-
-    def hc_copy(i, c_of, y_of):
-        slot = (c_of * 2 + y_of) * zs + (z - i + zs) % zs
-        k = (y_of + y) % 2 * zs + i
-        return slot, remote(hbuf.at[slot], hbuf.at[slot], hc_ss.at[k], hc_rs.at[k], other_core)
-
-    for i in range(1, zs):
-        hz_copy(i).start()
-
-    hy_copy(0, y)[1].start()
-    hc_copy(0, c, y)[1].start()
-    out_t[...] = jnp.zeros(out_t.shape, jnp.float32)
+    last = len(cuts) - 1
+    pieces = [pl.ds(sum(cuts[:i]), cuts[i]) for i in range(len(cuts))]
+    streams = [(p, y) for p in range(len(cuts))] + [(last, 1 - y)]
+
+    def slot_of(c_of, y_of, z_of):
+        return (c_of * 2 + y_of) * zs + z_of
+
+    def chain(stream, z_of, way):
+        piece, y_of = streams[stream]
+        ref = hbuf.at[slot_of(c, y_of, z_of), pieces[piece]]
+        return remote(ref, ref, hz_ss.at[(way * len(streams) + stream) * zs + z_of],
+                      hz_rs.at[stream * zs + z_of], dest((z + 1 - 2 * way + zs) % zs))
+
+    def across(piece, y_of, z_of):
+        ref = hbuf.at[slot_of(c, y_of, z_of), pieces[piece]]
+        k = piece * zs + z_of if piece < last else last * zs
+        return remote(ref, ref, hy_ss.at[k], hy_rs.at[k], other_y)
+
+    def pair(piece, c_of, y_of, z_of):
+        ref = hbuf.at[slot_of(c_of, y_of, z_of), pieces[piece]]
+        k = (piece * 2 + y_of) * zs + z_of
+        return remote(ref, ref, hc_ss.at[k], hc_rs.at[k], other_core)
 
     def take(slot):
         out_t[...] += (jnp.dot(hbuf[slot], hi_ref[slot], preferred_element_type=jnp.float32)
                        + jnp.dot(hbuf[slot], lo_ref[slot], preferred_element_type=jnp.float32))
 
+    def can_go(way):
+        return z + 1 < zs if way == 0 else z > 0
+
+    def both_ways(i, first, end, do):
+        for way in (0, 1):
+            z_of = z - i if way == 0 else z + i
+            there = (z_of >= 0) if way == 0 else (z_of < zs) & (i > 0)
+
+            @pl.when(there & (i >= first) & (i < end))
+            def _():
+                do(way, z_of)
+
+    def go_on(stream, z_of, way):
+        @pl.when(can_go(way))
+        def _():
+            chain(stream, z_of, way).start()
+
+    across(last, y, z).start()
+    for p in range(len(cuts)):
+        for way in (0, 1):
+            go_on(p, z, way)
+        if p < last:
+            across(p, y, z).start()
+    for p in range(len(cuts)):
+        pair(p, c, y, z).start()
+    out_t[...] = jnp.zeros(out_t.shape, jnp.float32)
     take(mine)
-
-    @pl.loop(1, zs)
+    across(last, 1 - y, z).wait_recv()
+    for way in (0, 1):
+        go_on(len(cuts), z, way)
+    pair(last, c, 1 - y, z).start()
+
+    @pl.loop(1, zs + 2)
     def _(i):
-        slot = hz_wait(i)
-        hy_copy(i, y)[1].start()
-        hc_copy(i, c, y)[1].start()
-        take(slot)
-
-    @pl.loop(0, zs)
-    def _(i):
-        slot, copy = hy_copy(i, 1 - y)
-        copy.wait_recv()
-        hc_copy(i, c, 1 - y)[1].start()
-        take(slot)
-
-    @pl.loop(0, 2 * zs)
-    def _(k):
-        slot, copy = hc_copy(k % zs, 1 - c, (k // zs + y) % 2)
-        copy.wait_recv()
-        take(slot)
-
-    out_ref[...] = out_t[...].T
+        for stream in range(len(streams)):
+            def arrive(way, z_of):
+                chain(stream, z_of, way).wait_recv()
+                go_on(stream, z_of, way)
+                piece, y_of = streams[stream]
+                if piece < last:
+                    across(piece, y, z_of).start()
+                pair(piece, c, y_of, z_of).start()
+
+            both_ways(i, 1, zs, arrive)
+
+        both_ways(i, 1, zs, lambda way, z_of: take(slot_of(c, y, z_of)))
+
+        def far(way, z_of):
+            for p in range(last):
+                across(p, 1 - y, z_of).wait_recv()
+                pair(p, c, 1 - y, z_of).start()
+            take(slot_of(c, 1 - y, z_of))
+
+        both_ways(i - 1, 0, zs, far)
+
+        def other(way, z_of):
+            for y_of in (y, 1 - y):
+                for p in range(len(cuts)):
+                    pair(p, 1 - c, y_of, z_of).wait_recv()
+                take(slot_of(1 - c, y_of, z_of))
+
+        both_ways(i - 2, 0, zs, other)
+
+    out_ref[...] = out_t[...]
 
     @pl.loop(0, 2 * zs)
     def _(j):
@@ -203,13 +252,23 @@
     @pl.loop(1, zs)
     def _(i):
         z_copy(i).wait_send()
-        hz_copy(i).wait_send()
+
+    across(last, y, z).wait_send()
 
     @pl.loop(0, zs)
-    def _(i):
-        hy_copy(i, y)[1].wait_send()
-        hc_copy(i, c, y)[1].wait_send()
-        hc_copy(i, c, 1 - y)[1].wait_send()
+    def _(k):
+        for p in range(len(cuts)):
+            if p < last:
+                across(p, y, k).wait_send()
+            for y_of in (0, 1):
+                pair(p, c, y_of, k).wait_send()
+        for way in (0, 1):
+            from_there = k <= z if way == 0 else k >= z
+
+            @pl.when(can_go(way) & from_there)
+            def _():
+                for stream in range(len(streams)):
+                    chain(stream, k, way).wait_send()
 
 
 def solution(mesh):
@@ -220,27 +279,35 @@
              weight):
         nb, bs = block_values.shape[:2]
         rows, width = features.shape
-        smem = pl.BlockSpec(memory_space=pltpu.SMEM)
+        anywhere = pl.BlockSpec(memory_space=pl.ANY)
+        vmem_limit = (n + 6) * 7 // 8 * MIB
         vmem = pl.BlockSpec(memory_space=pltpu.VMEM)
+        owner = block_owner[:, 0]
+        place = (owner % 2 * 2 + owner // 2 % 2) * zs + owner // 4
+        index = ((place * 2 + block_sub) * 2 + block_col) * 2 + block_valid
         blocks = jax.ShapeDtypeStruct((n, rows, rows), jnp.bfloat16)
         hi, lo = pl.pallas_call(
-            functools.partial(merge_kernel, n, bs, nb),
+            functools.partial(merge_kernel, bs, nb),
             out_shape=(blocks, blocks),
-            in_specs=[smem] * 4 + [pl.BlockSpec(memory_space=pl.ANY)],
+            in_specs=[anywhere] * 2,
             out_specs=(vmem, vmem),
             scratch_shapes=[
                 pltpu.VMEM((n, rows, rows), jnp.float32),
                 pltpu.VMEM((nb, bs, bs), jnp.bfloat16),
+                pltpu.SMEM((nb,), jnp.int32),
                 pltpu.SemaphoreType.DMA((CHUNKS,)),
+                pltpu.SemaphoreType.DMA,
             ],
-            compiler_params=pltpu.CompilerParams(vmem_limit_bytes=44 * MIB),
-        )(block_owner[:, 0], block_sub, block_col, block_valid, block_values)
+            compiler_params=pltpu.CompilerParams(vmem_limit_bytes=vmem_limit),
+        )(index, block_values)
 
         f32, bf16 = jnp.float32, jnp.bfloat16
+        cuts = tuple(width // 16 * part for part in CUTS)
+        count = len(cuts)
         dma = pltpu.SemaphoreType.DMA
         return pl.pallas_call(
-            functools.partial(layer_kernel, n),
-            out_shape=jax.ShapeDtypeStruct((rows, width), f32),
+            functools.partial(layer_kernel, n, cuts),
+            out_shape=jax.ShapeDtypeStruct((width, rows), f32),
             in_specs=[vmem] * 5,
             out_specs=vmem,
             scratch_shapes=[
@@ -255,11 +322,13 @@
                 pltpu.VMEM((n, width, rows), bf16),
                 pltpu.VMEM((width, rows), f32),
                 dma((2 * zs,)), dma((2 * zs,)), dma((zs,)), dma((zs,)), dma((zs,)), dma((zs,)),
-                dma((zs,)), dma((zs,)), dma((zs,)), dma((zs,)), dma((2 * zs,)), dma((2 * zs,)),
+                dma((2 * (count + 1) * zs,)), dma(((count + 1) * zs,)),
+                dma(((count - 1) * zs + 1,)), dma(((count - 1) * zs + 1,)),
+                dma((2 * count * zs,)), dma((2 * count * zs,)),
             ],
             compiler_params=pltpu.CompilerParams(
-                collective_id=0, has_side_effects=True, vmem_limit_bytes=60 * MIB),
-        )(hi, lo, features, norm_gain[None, :], weight)
+                collective_id=0, has_side_effects=True, vmem_limit_bytes=vmem_limit),
+        )(hi, lo, features, norm_gain[None, :], weight).T
 
     placed = (
         P(("groups", "col"), None),

time: 63.6 us -> 52.7 us (0.83)
  the two profiles are of different devices: /device:TPU:20 before, /device:TPU:0 now
where the time goes in v3:
time: 52.7 us; the launch traced here: 52.5 us
  Pallas kernels  48.7 us (92%)
  local copies, waits for them, and re-layouts  3.03 us (6%)
  other arithmetic  0.73 us (1%)
    pallas_call x1, Pallas kernels, body(): pl.pallas_call(functools.partial(layer_kernel, n, cuts), out_shape=jax.Sh...  43.7 us
    pallas_call x1, Pallas kernels, body(): pl.pallas_call(functools.partial(merge_kernel, bs, nb), out_shape=(blocks...  5.04 us
    unnamed x8, local copies, waits for them, and re-layouts  2.19 us

profile of v3, /device:TPU:0, one launch (start us, length us, event | category | flops | bytes accessed | tf_op | source)
XLA Modules:
  0.0 52.5 jit_solution(11172641591621652317)
XLA Ops:
  0.0 0.7 %multiply_add_fusion.index_any = s32[128]{0:T(128)S(1)} fusion(s32[128]{0:T(128)} %param.13, s32[128]{0:T(128)} %param.12, s32[128]{0:T(128)} %param.11, s32[128,1]{0,1:T(1,128)} %param.10), kind=kLoop, calls=%fused_computation.16 | loop fusion | flops 6400 | bytes 2560 | tf_op jit(solution)/shard_map/add | solution.py:287
  0.7 0.0 copy-start
  0.7 2.2 %copy-done = bf16[128,128,128]{2,1,0:T(8,128)(2,1)S(1)} copy-done((bf16[128,128,128]{2,1,0:T(8,128)(2,1)S(1)}, bf16[128,128,128]{2,1,0:T(8,128)(2,1)}, u32[]{:S(2)}) %copy-start) | copy-done | bytes 4194328
  2.9 0.0 copy-start.1
  2.9 0.0 copy-start.2
  2.9 0.0 copy-start.3
  2.9 5.0 %shard_map.82 = (bf16[16,256,256]{2,1,0:T(8,128)(2,1)S(1)}, bf16[16,256,256]{2,1,0:T(8,128)(2,1)S(1)}) custom-call(s32[128]{0:T(128)S(1)} %multiply_add_fusion.index_any, bf16[128,128,128]{2,1,0:T(8,128)(2,1)S(1)} %copy-done), custom_call_target="tpu_custom_call" | custom-call | tf_op jit(solution)/shard_map/pallas_call | solution.py:289
  8.0 0.0 copy-done.1
  8.0 0.0 copy-done.2
  8.0 0.0 copy-done.3
  8.0 43.7 %shard_map.83 = f32[256,256]{1,0:T(8,128)S(1)} custom-call(bf16[16,256,256]{2,1,0:T(8,128)(2,1)S(1)} %get-tuple-element.7.hi_ref, bf16[16,256,256]{2,1,0:T(8,128)(2,1)S(1)} %get-tuple-element.8.lo_ref, bf16[256,256]{1,0:T(8,128)(2,1)S(1)} %copy-done.1, f32[1,256]{1,0:T(1,128)S(1)} %bitcast.19, bf16[256,256]{1,0:T(8,128)(2,1)S(1)} %copy-done.2), custom_call_target="tpu_custom_call" | custom-call | tf_op jit(solution)/shard_map/pallas_call | solution.py:308
  51.7 0.8 %copy.9 = f32[256,256]{1,0:T(8,128)} copy(f32[256,256]{0,1:T(8,128)S(1)} %bitcast.18) | data formatting | bytes 524288 | tf_op jit(solution)/shard_map/transpose | solution.py:331
Async XLA Ops:
  0.7 2.2 %copy-start = (bf16[128,128,128]{2,1,0:T(8,128)(2,1)S(1)}, bf16[128,128,128]{2,1,0:T(8,128)(2,1)}, u32[]{:S(2)}) copy-start(bf16[128,128,128]{2,1,0:T(8,128)(2,1)} %values_ref.1) | copy-start | bytes 12582916
  2.9 5.1 %copy-start.1 = (bf16[256,256]{1,0:T(8,128)(2,1)S(1)}, bf16[256,256]{1,0:T(8,128)(2,1)}, u32[]{:S(2)}) copy-start(bf16[256,256]{1,0:T(8,128)(2,1)} %x_ref.1) | copy-start | bytes 393220
  2.9 5.1 %copy-start.2 = (bf16[256,256]{1,0:T(8,128)(2,1)S(1)}, bf16[256,256]{1,0:T(8,128)(2,1)}, u32[]{:S(2)}) copy-start(bf16[256,256]{1,0:T(8,128)(2,1)} %w_ref.1) | copy-start | bytes 393220
  2.9 5.1 %copy-start.3 = (f32[256]{0:T(256)S(1)}, f32[256]{0:T(256)}, u32[]{:S(2)}) copy-start(f32[256]{0:T(256)} %param.14) | copy-start | bytes 3076

commit v4 on v3

--- a/solution.py
+++ b/solution.py
@@ -88,58 +88,69 @@
     def core_copy(j):
         return remote(pa_send.at[j], pa_recv.at[j], pa_ss.at[j], pa_rs.at[j], other_core)
 
-    def turned(k):
-        return (k + (1 - y) * zs) % (2 * zs)
-
-    @pl.loop(0, 2 * zs)
-    def _(k):
-        j = turned(k)
+    @pl.loop(0, zs)
+    def _(k):
+        j = (1 - y) * zs + (z + 1 + k) % zs
         pa_send[j] = product((1 - c) * 2 * zs + j)
 
     pl.semaphore_wait(barrier, zs + 1)
 
-    @pl.loop(0, 2 * zs)
-    def _(k):
-        core_copy(turned(k)).start()
-
-    @pl.loop(0, 2 * zs)
-    def _(k):
-        j = turned(k)
-        acc[j] = product(c * 2 * zs + j)
-
-    def y_copy(k):
-        return remote(yb_send.at[k], yb_recv.at[k], yb_ss.at[k], yb_rs.at[k], other_y)
+    @pl.loop(0, zs)
+    def _(k):
+        core_copy((1 - y) * zs + (z + 1 + k) % zs).start()
+
+    half = acc.shape[1] // 2
+    halves = (pl.ds(0, half), pl.ds(half, half))
+
+    def y_copy(k, h):
+        return remote(yb_send.at[k, halves[h]], yb_recv.at[k, halves[h]],
+                      yb_ss.at[2 * k + h], yb_rs.at[2 * k + h], other_y)
 
     @pl.loop(0, zs)
     def _(k):
         k = (z + 1 + k) % zs
         j = (1 - y) * zs + k
+        acc[j] = product(c * 2 * zs + j)
         core_copy(j).wait_recv()
-        yb_send[k] = (acc[j] + pa_recv[j]).astype(jnp.bfloat16)
-        y_copy(k).start()
-
-    @pl.loop(0, zs)
-    def _(k):
-        j = y * zs + k
+        for h in (0, 1):
+            yb_send[k, halves[h]] = (acc[j, halves[h]] + pa_recv[j, halves[h]]).astype(jnp.bfloat16)
+            y_copy(k, h).start()
+
+    @pl.loop(0, zs)
+    def _(k):
+        j = y * zs + (z + 1 + k) % zs
+        pa_send[j] = product((1 - c) * 2 * zs + j)
+        core_copy(j).start()
+
+    @pl.loop(0, zs)
+    def _(k):
+        j = y * zs + (z + 1 + k) % zs
+        acc[j] = product(c * 2 * zs + j)
         core_copy(j).wait_recv()
         acc[j] = acc[j] + pa_recv[j]
 
-    def z_copy(i):
-        return remote(zb_send.at[i], zb_recv.at[i], zb_ss.at[i], zb_rs.at[i], dest((z + i) % zs))
+    def z_copy(i, h):
+        return remote(zb_send.at[i, halves[h]], zb_recv.at[i, halves[h]],
+                      zb_ss.at[2 * i + h], zb_rs.at[2 * i + h], dest((z + i) % zs))
 
     @pl.loop(1, zs)
     def _(i):
         k = (z + i) % zs
-        y_copy(k).wait_recv()
-        zb_send[i] = (acc[y * zs + k] + yb_recv[k].astype(jnp.float32)).astype(jnp.bfloat16)
-        z_copy(i).start()
-
-    y_copy(z).wait_recv()
+        for h in (0, 1):
+            y_copy(k, h).wait_recv()
+            zb_send[i, halves[h]] = (
+                acc[y * zs + k, halves[h]] + yb_recv[k, halves[h]].astype(jnp.float32)
+            ).astype(jnp.bfloat16)
+            z_copy(i, h).start()
+
+    for h in (0, 1):
+        y_copy(z, h).wait_recv()
     agg[...] = acc[y * zs + z] + yb_recv[z].astype(jnp.float32)
 
     @pl.loop(1, zs)
     def _(i):
-        z_copy(i).wait_recv()
+        for h in (0, 1):
+            z_copy(i, h).wait_recv()
         agg[...] += zb_recv[i].astype(jnp.float32)
 
     total = agg[...]
@@ -247,11 +258,13 @@
 
     @pl.loop(0, zs)
     def _(k):
-        y_copy(k).wait_send()
+        for h in (0, 1):
+            y_copy(k, h).wait_send()
 
     @pl.loop(1, zs)
     def _(i):
-        z_copy(i).wait_send()
+        for h in (0, 1):
+            z_copy(i, h).wait_send()
 
     across(last, y, z).wait_send()
 
@@ -321,7 +334,8 @@
                 pltpu.VMEM((rows, width), f32),
                 pltpu.VMEM((n, width, rows), bf16),
                 pltpu.VMEM((width, rows), f32),
-                dma((2 * zs,)), dma((2 * zs,)), dma((zs,)), dma((zs,)), dma((zs,)), dma((zs,)),
+                dma((2 * zs,)), dma((2 * zs,)), dma((2 * zs,)), dma((2 * zs,)), dma((2 * zs,)),
+                dma((2 * zs,)),
                 dma((2 * (count + 1) * zs,)), dma(((count + 1) * zs,)),
                 dma(((count - 1) * zs + 1,)), dma(((count - 1) * zs + 1,)),
                 dma((2 * count * zs,)), dma((2 * count * zs,)),

time: 52.7 us -> 50.7 us (0.962)
  Pallas kernels: 48.7 us -> 46.7 us
    pallas_call x1, Pallas kernels: 43.7 us -> 41.7 us  [body(): pl.pallas_call(functools.partial(layer_kernel, n, cuts), out_shape=jax.Sh...]
where the time goes in v4:
time: 50.7 us; the launch traced here: 50.5 us
  Pallas kernels  46.7 us (92%)
  local copies, waits for them, and re-layouts  3.03 us (6%)
  other arithmetic  0.73 us (1%)
    pallas_call x1, Pallas kernels, body(): pl.pallas_call(functools.partial(layer_kernel, n, cuts), out_shape=jax.Sh...  41.7 us
    pallas_call x1, Pallas kernels, body(): pl.pallas_call(functools.partial(merge_kernel, bs, nb), out_shape=(blocks...  5.04 us
    unnamed x8, local copies, waits for them, and re-layouts  2.19 us

profile of v4, /device:TPU:0, one launch (start us, length us, event | category | flops | bytes accessed | tf_op | source)
XLA Modules:
  0.0 50.5 jit_solution(14289008488106233816)
XLA Ops:
  0.0 0.7 %multiply_add_fusion.index_any = s32[128]{0:T(128)S(1)} fusion(s32[128]{0:T(128)} %param.13, s32[128]{0:T(128)} %param.12, s32[128]{0:T(128)} %param.11, s32[128,1]{0,1:T(1,128)} %param.10), kind=kLoop, calls=%fused_computation.16 | loop fusion | flops 6400 | bytes 2560 | tf_op jit(solution)/shard_map/add | solution.py:300
  0.7 0.0 copy-start
  0.7 2.2 %copy-done = bf16[128,128,128]{2,1,0:T(8,128)(2,1)S(1)} copy-done((bf16[128,128,128]{2,1,0:T(8,128)(2,1)S(1)}, bf16[128,128,128]{2,1,0:T(8,128)(2,1)}, u32[]{:S(2)}) %copy-start) | copy-done | bytes 4194328
  2.9 0.0 copy-start.1
  2.9 0.0 copy-start.2
  2.9 0.0 copy-start.3
  2.9 5.0 %shard_map.82 = (bf16[16,256,256]{2,1,0:T(8,128)(2,1)S(1)}, bf16[16,256,256]{2,1,0:T(8,128)(2,1)S(1)}) custom-call(s32[128]{0:T(128)S(1)} %multiply_add_fusion.index_any, bf16[128,128,128]{2,1,0:T(8,128)(2,1)S(1)} %copy-done), custom_call_target="tpu_custom_call" | custom-call | tf_op jit(solution)/shard_map/pallas_call | solution.py:302
  8.0 0.0 copy-done.1
  8.0 0.0 copy-done.2
  8.0 0.0 copy-done.3
  8.0 41.7 %shard_map.83 = f32[256,256]{1,0:T(8,128)S(1)} custom-call(bf16[16,256,256]{2,1,0:T(8,128)(2,1)S(1)} %get-tuple-element.7.hi_ref, bf16[16,256,256]{2,1,0:T(8,128)(2,1)S(1)} %get-tuple-element.8.lo_ref, bf16[256,256]{1,0:T(8,128)(2,1)S(1)} %copy-done.1, f32[1,256]{1,0:T(1,128)S(1)} %bitcast.19, bf16[256,256]{1,0:T(8,128)(2,1)S(1)} %copy-done.2), custom_call_target="tpu_custom_call" | custom-call | tf_op jit(solution)/shard_map/pallas_call | solution.py:321
  49.7 0.8 %copy.9 = f32[256,256]{1,0:T(8,128)} copy(f32[256,256]{0,1:T(8,128)S(1)} %bitcast.18) | data formatting | bytes 524288 | tf_op jit(solution)/shard_map/transpose | solution.py:345
Async XLA Ops:
  0.7 2.2 %copy-start = (bf16[128,128,128]{2,1,0:T(8,128)(2,1)S(1)}, bf16[128,128,128]{2,1,0:T(8,128)(2,1)}, u32[]{:S(2)}) copy-start(bf16[128,128,128]{2,1,0:T(8,128)(2,1)} %values_ref.1) | copy-start | bytes 12582916
  2.9 5.1 %copy-start.1 = (bf16[256,256]{1,0:T(8,128)(2,1)S(1)}, bf16[256,256]{1,0:T(8,128)(2,1)}, u32[]{:S(2)}) copy-start(bf16[256,256]{1,0:T(8,128)(2,1)} %x_ref.1) | copy-start | bytes 393220
  2.9 5.1 %copy-start.2 = (bf16[256,256]{1,0:T(8,128)(2,1)S(1)}, bf16[256,256]{1,0:T(8,128)(2,1)}, u32[]{:S(2)}) copy-start(bf16[256,256]{1,0:T(8,128)(2,1)} %w_ref.1) | copy-start | bytes 393220
  2.9 5.1 %copy-start.3 = (f32[256]{0:T(256)S(1)}, f32[256]{0:T(256)}, u32[]{:S(2)}) copy-start(f32[256]{0:T(256)} %param.14) | copy-start | bytes 3076

commit v5 on v4

--- a/solution.py
+++ b/solution.py
@@ -35,13 +35,13 @@
     for i in range(CHUNKS):
         chunk(i).wait()
 
-        @pl.loop(i * per, (i + 1) * per)
+        @pl.loop(i * per, (i + 1) * per, unroll=4)
         def _(s):
             index = index_ref[s]
-            place = index // 8
-            rows = pl.ds(pl.multiple_of(index // 4 % 2 * bs, bs), bs)
-            columns = pl.ds(pl.multiple_of(index // 2 % 2 * bs, bs), bs)
-            live = (index % 2).astype(jnp.float32)
+            place = index >> 3
+            rows = pl.ds(pl.multiple_of((index >> 2 & 1) * bs, bs), bs)
+            columns = pl.ds(pl.multiple_of((index >> 1 & 1) * bs, bs), bs)
+            live = (index & 1).astype(jnp.float32)
             dense[place, rows, columns] += staged[s].astype(jnp.float32) * live
 
     @pl.loop(0, n)

time: 50.7 us -> 48.2 us (0.951)
  Pallas kernels: 46.7 us -> 44.2 us
    pallas_call x1, Pallas kernels: 5.04 us -> 2.57 us  [body(): pl.pallas_call(functools.partial(merge_kernel, bs, nb), out_shape=(blocks...]
where the time goes in v5:
time: 48.2 us; the launch traced here: 48.1 us
  Pallas kernels  44.2 us (92%)
  local copies, waits for them, and re-layouts  3.03 us (6%)
  other arithmetic  0.73 us (2%)
    pallas_call x1, Pallas kernels, body(): pl.pallas_call(functools.partial(layer_kernel, n, cuts), out_shape=jax.Sh...  41.7 us
    pallas_call x1, Pallas kernels, body(): pl.pallas_call(functools.partial(merge_kernel, bs, nb), out_shape=(blocks...  2.57 us
    unnamed x8, local copies, waits for them, and re-layouts  2.19 us

profile of v5, /device:TPU:0, one launch (start us, length us, event | category | flops | bytes accessed | tf_op | source)
XLA Modules:
  0.0 48.1 jit_solution(715542757796463686)
XLA Ops:
  0.0 0.7 %multiply_add_fusion.index_any = s32[128]{0:T(128)S(1)} fusion(s32[128]{0:T(128)} %param.13, s32[128]{0:T(128)} %param.12, s32[128]{0:T(128)} %param.11, s32[128,1]{0,1:T(1,128)} %param.10), kind=kLoop, calls=%fused_computation.16 | loop fusion | flops 6400 | bytes 2560 | tf_op jit(solution)/shard_map/add | solution.py:300
  0.7 0.0 copy-start
  0.7 2.2 %copy-done = bf16[128,128,128]{2,1,0:T(8,128)(2,1)S(1)} copy-done((bf16[128,128,128]{2,1,0:T(8,128)(2,1)S(1)}, bf16[128,128,128]{2,1,0:T(8,128)(2,1)}, u32[]{:S(2)}) %copy-start) | copy-done | bytes 4194328
  2.9 0.0 copy-start.1
  2.9 0.0 copy-start.2
  2.9 0.0 copy-start.3
  2.9 2.6 %shard_map.82 = (bf16[16,256,256]{2,1,0:T(8,128)(2,1)S(1)}, bf16[16,256,256]{2,1,0:T(8,128)(2,1)S(1)}) custom-call(s32[128]{0:T(128)S(1)} %multiply_add_fusion.index_any, bf16[128,128,128]{2,1,0:T(8,128)(2,1)S(1)} %copy-done), custom_call_target="tpu_custom_call" | custom-call | tf_op jit(solution)/shard_map/pallas_call | solution.py:302
  5.5 0.0 copy-done.1
  5.5 0.0 copy-done.2
  5.5 0.0 copy-done.3
  5.5 41.7 %shard_map.83 = f32[256,256]{1,0:T(8,128)S(1)} custom-call(bf16[16,256,256]{2,1,0:T(8,128)(2,1)S(1)} %get-tuple-element.7.hi_ref, bf16[16,256,256]{2,1,0:T(8,128)(2,1)S(1)} %get-tuple-element.8.lo_ref, bf16[256,256]{1,0:T(8,128)(2,1)S(1)} %copy-done.1, f32[1,256]{1,0:T(1,128)S(1)} %bitcast.19, bf16[256,256]{1,0:T(8,128)(2,1)S(1)} %copy-done.2), custom_call_target="tpu_custom_call" | custom-call | tf_op jit(solution)/shard_map/pallas_call | solution.py:321
  47.2 0.8 %copy.9 = f32[256,256]{1,0:T(8,128)} copy(f32[256,256]{0,1:T(8,128)S(1)} %bitcast.18) | data formatting | bytes 524288 | tf_op jit(solution)/shard_map/transpose | solution.py:345
Async XLA Ops:
  0.7 2.2 %copy-start = (bf16[128,128,128]{2,1,0:T(8,128)(2,1)S(1)}, bf16[128,128,128]{2,1,0:T(8,128)(2,1)}, u32[]{:S(2)}) copy-start(bf16[128,128,128]{2,1,0:T(8,128)(2,1)} %values_ref.1) | copy-start | bytes 12582916
  2.9 2.6 %copy-start.1 = (bf16[256,256]{1,0:T(8,128)(2,1)S(1)}, bf16[256,256]{1,0:T(8,128)(2,1)}, u32[]{:S(2)}) copy-start(bf16[256,256]{1,0:T(8,128)(2,1)} %x_ref.1) | copy-start | bytes 393220
  2.9 2.6 %copy-start.2 = (bf16[256,256]{1,0:T(8,128)(2,1)S(1)}, bf16[256,256]{1,0:T(8,128)(2,1)}, u32[]{:S(2)}) copy-start(bf16[256,256]{1,0:T(8,128)(2,1)} %w_ref.1) | copy-start | bytes 393220
  2.9 2.6 %copy-start.3 = (f32[256]{0:T(256)S(1)}, f32[256]{0:T(256)}, u32[]{:S(2)}) copy-start(f32[256]{0:T(256)} %param.14) | copy-start | bytes 3076

commit v6 on v5

--- a/solution.py
+++ b/solution.py
@@ -35,7 +35,7 @@
     for i in range(CHUNKS):
         chunk(i).wait()
 
-        @pl.loop(i * per, (i + 1) * per, unroll=4)
+        @pl.loop(i * per, (i + 1) * per, unroll=8)
         def _(s):
             index = index_ref[s]
             place = index >> 3

time: 48.2 us -> 48.2 us (level)
  no operation moved by 1% of the time
where the time goes in v6:
time: 48.2 us; the launch traced here: 48 us
  Pallas kernels  44.2 us (92%)
  local copies, waits for them, and re-layouts  3.03 us (6%)
  other arithmetic  0.73 us (2%)
    pallas_call x1, Pallas kernels, body(): pl.pallas_call(functools.partial(layer_kernel, n, cuts), out_shape=jax.Sh...  41.7 us
    pallas_call x1, Pallas kernels, body(): pl.pallas_call(functools.partial(merge_kernel, bs, nb), out_shape=(blocks...  2.54 us
    unnamed x8, local copies, waits for them, and re-layouts  2.19 us

profile of v6, /device:TPU:0, one launch (start us, length us, event | category | flops | bytes accessed | tf_op | source)
XLA Modules:
  0.0 48.0 jit_solution(9476672055158111846)
XLA Ops:
  0.0 0.7 %multiply_add_fusion.index_any = s32[128]{0:T(128)S(1)} fusion(s32[128]{0:T(128)} %param.13, s32[128]{0:T(128)} %param.12, s32[128]{0:T(128)} %param.11, s32[128,1]{0,1:T(1,128)} %param.10), kind=kLoop, calls=%fused_computation.16 | loop fusion | flops 6400 | bytes 2560 | tf_op jit(solution)/shard_map/add | solution.py:300
  0.7 0.0 copy-start
  0.7 2.2 %copy-done = bf16[128,128,128]{2,1,0:T(8,128)(2,1)S(1)} copy-done((bf16[128,128,128]{2,1,0:T(8,128)(2,1)S(1)}, bf16[128,128,128]{2,1,0:T(8,128)(2,1)}, u32[]{:S(2)}) %copy-start) | copy-done | bytes 4194328
  2.9 0.0 copy-start.1
  2.9 0.0 copy-start.2
  2.9 0.0 copy-start.3
  2.9 2.5 %shard_map.82 = (bf16[16,256,256]{2,1,0:T(8,128)(2,1)S(1)}, bf16[16,256,256]{2,1,0:T(8,128)(2,1)S(1)}) custom-call(s32[128]{0:T(128)S(1)} %multiply_add_fusion.index_any, bf16[128,128,128]{2,1,0:T(8,128)(2,1)S(1)} %copy-done), custom_call_target="tpu_custom_call" | custom-call | tf_op jit(solution)/shard_map/pallas_call | solution.py:302
  5.5 0.0 copy-done.1
  5.5 0.0 copy-done.2
  5.5 0.0 copy-done.3
  5.5 41.7 %shard_map.83 = f32[256,256]{1,0:T(8,128)S(1)} custom-call(bf16[16,256,256]{2,1,0:T(8,128)(2,1)S(1)} %get-tuple-element.7.hi_ref, bf16[16,256,256]{2,1,0:T(8,128)(2,1)S(1)} %get-tuple-element.8.lo_ref, bf16[256,256]{1,0:T(8,128)(2,1)S(1)} %copy-done.1, f32[1,256]{1,0:T(1,128)S(1)} %bitcast.19, bf16[256,256]{1,0:T(8,128)(2,1)S(1)} %copy-done.2), custom_call_target="tpu_custom_call" | custom-call | tf_op jit(solution)/shard_map/pallas_call | solution.py:321
  47.2 0.8 %copy.9 = f32[256,256]{1,0:T(8,128)} copy(f32[256,256]{0,1:T(8,128)S(1)} %bitcast.18) | data formatting | bytes 524288 | tf_op jit(solution)/shard_map/transpose | solution.py:345
Async XLA Ops:
  0.7 2.2 %copy-start = (bf16[128,128,128]{2,1,0:T(8,128)(2,1)S(1)}, bf16[128,128,128]{2,1,0:T(8,128)(2,1)}, u32[]{:S(2)}) copy-start(bf16[128,128,128]{2,1,0:T(8,128)(2,1)} %values_ref.1) | copy-start | bytes 12582916
  2.9 2.6 %copy-start.1 = (bf16[256,256]{1,0:T(8,128)(2,1)S(1)}, bf16[256,256]{1,0:T(8,128)(2,1)}, u32[]{:S(2)}) copy-start(bf16[256,256]{1,0:T(8,128)(2,1)} %x_ref.1) | copy-start | bytes 393220
  2.9 2.6 %copy-start.2 = (bf16[256,256]{1,0:T(8,128)(2,1)S(1)}, bf16[256,256]{1,0:T(8,128)(2,1)}, u32[]{:S(2)}) copy-start(bf16[256,256]{1,0:T(8,128)(2,1)} %w_ref.1) | copy-start | bytes 393220
  2.9 2.6 %copy-start.3 = (f32[256]{0:T(256)S(1)}, f32[256]{0:T(256)}, u32[]{:S(2)}) copy-start(f32[256]{0:T(256)} %param.14) | copy-start | bytes 3076
